TPU v7x, 32 devices: a whole 2x2x4 slice. The times are simulated.
32 devices in a mesh: groups: 2 (over y), row: 8 (over z, x), col: 2 (over core).
Axes of the slice: x: 2, y: 2, z: 4, core: 2. Of those that a mesh axis runs over, the one named last changes fastest.
Arguments:
- iterate: bfloat16 [16384, 3584], P(('groups', 'row'), 'col'), parts along dimension 0, may hold values from -6 to 6
Outputs:
- updated: bfloat16 [16384, 3584], P(('groups', 'row'), 'col'), parts along dimension 0
There are 2 independent parts, one for each index of `groups`. A program takes and returns all parts, laid end to end along the dimension named above; each array names one. Nothing has to cross between parts.
All inputs are finite; a program needn't handle non-finite values.
Results may differ from a plain program's by a relative error of at most 0.0049.
Values may be sent and summed in bfloat16 or wider, within the bound.
No kernel may reach another device: no remote copies, remote signals or barrier semaphores. Data moves between devices by JAX's collectives and lax.ppermute only.
A program may use at most 128 MiB of HBM per device.

v0:
```python
import functools

import jax
import jax.numpy as jnp
from jax import lax
from jax.experimental import pallas as pl
from jax.experimental.pallas import tpu as pltpu
from jax.sharding import PartitionSpec as P

R = 8192

coef_linear = 3.4445
coef_cubic = -4.775
coef_quintic = 2.0315

PANEL = 256
RING_MOST = 16
STEP_BYTES = 20 * 2**20
STEP_FLOPS = 8 * 10**9
F32 = jnp.float32
BF16 = jnp.bfloat16


def dot(a, b, ca, cb):
    return lax.dot_general(a, b, (((ca,), (cb,)), ((), ())), preferred_element_type=F32)


def emit_chunk(start, o_ref, chunk_refs):
    for i, ref in enumerate(chunk_refs):
        size = ref.shape[0]
        ref[...] = o_ref[pl.ds(pl.multiple_of(start + i * size, 16), size), :]


def diag_kernel(place_ref, x_ref, o_ref, *refs):
    chunk_refs, wide = refs[:-1], refs[-1]
    half = x_ref.shape[1]
    width = o_ref.shape[1]
    wide[:, :half] = x_ref[...]
    wide[:, half:] = x_ref[:, : width - PANEL]
    for at in range(0, half, PANEL):
        strip = dot(x_ref[:, at : at + PANEL], wide[:, at : at + width], 0, 0)
        o_ref[at : at + PANEL, :] = (strip * (1.0 / R)).astype(BF16)
    emit_chunk(place_ref[0], o_ref, chunk_refs)


def gram_outs(half, width, size):
    return [jax.ShapeDtypeStruct((n, width), BF16) for n in ([half] if size is None else [half, size // 2, size // 2])]


def diag_gram(x, width, start, size):
    rows, half = x.shape
    outs = gram_outs(half, width, size)
    vmem = pl.BlockSpec(memory_space=pltpu.VMEM)
    return pl.pallas_call(
        diag_kernel,
        out_shape=outs,
        in_specs=[pl.BlockSpec(memory_space=pltpu.SMEM), vmem],
        out_specs=[vmem] * len(outs),
        scratch_shapes=[pltpu.VMEM((rows, half + width - PANEL), BF16)],
        compiler_params=pltpu.CompilerParams(vmem_limit_bytes=40 * 2**20),
        cost_estimate=pl.CostEstimate(flops=2 * rows * half * width, bytes_accessed=4 * rows * half, transcendentals=0),
    )(start.reshape(1), x)


def side_kernel(outs, place_ref, own_ref, other_ref, *refs):
    o_ref, chunk_refs = refs[-outs], refs[len(refs) - outs + 1 :]
    half = own_ref.shape[1]
    part = half // 2

    def go(left_ref, right_ref, start):
        for at in range(0, half, PANEL):
            strip = dot(left_ref[:, at : at + PANEL], right_ref[:, start : start + part], 0, 0)
            o_ref[at : at + PANEL, :] = (strip * (1.0 / R)).astype(BF16)

    @pl.when(place_ref[1] == 0)
    def _():
        go(own_ref, other_ref, 0)

    @pl.when(place_ref[1] == 1)
    def _():
        go(other_ref, own_ref, part)

    emit_chunk(place_ref[0], o_ref, chunk_refs)


def side_gram(core, own, other, start, size):
    rows, half = own.shape
    outs = gram_outs(half, half // 2, size)
    vmem = pl.BlockSpec(memory_space=pltpu.VMEM)
    return pl.pallas_call(
        functools.partial(side_kernel, len(outs)),
        out_shape=outs,
        in_specs=[pl.BlockSpec(memory_space=pltpu.SMEM), vmem, vmem],
        out_specs=[vmem] * len(outs),
        compiler_params=pltpu.CompilerParams(vmem_limit_bytes=40 * 2**20),
        cost_estimate=pl.CostEstimate(flops=STEP_FLOPS, bytes_accessed=6 * rows * half, transcendentals=0),
    )(jnp.stack([start, core]), own, other)


def finish_kernel(panels, reach, part, pieces, place_ref, *refs):
    own_ref, other_ref = refs[:2]
    piece_refs = refs[2 : 2 + 2 * sum(pieces)]
    keep_ref, send_ref, xe, ye, yf, diag, side, out, sems = refs[2 + 2 * sum(pieces) :]
    core = place_ref[0]
    rows = xe.shape[1]
    half = panels * PANEL
    width = reach * PANEL

    copies = []

    def bring(source, target):
        copy = pltpu.make_async_copy(source, target, sems.at[len(copies)])
        copy.start()
        copies.append(copy)

    mine = pl.ds(pl.multiple_of(core * rows, rows), rows)
    bring(own_ref.at[mine, :], xe.at[core, :, pl.ds(0, half)])
    bring(other_ref.at[mine, :], xe.at[1 - core, :, pl.ds(0, half)])
    at = 0
    for owner in (core, 1 - core):
        for k, store in enumerate((diag, side)):
            for m in range(pieces[k]):
                piece = piece_refs[at]
                start = place_ref[1 + m + (pieces[0] if k == 1 else 0)]
                start = pl.multiple_of(start, 16)
                bring(piece, store.at[owner, pl.ds(start, piece.shape[0]), :])
                at += 1
    early = 2 + pieces[0]
    late = early + pieces[1]
    diag_copies = copies[:early] + copies[late : late + pieces[0]]
    side_copies = copies[early:late] + copies[late + pieces[0] :]

    def around(src, h, j):
        at = pl.multiple_of(j * PANEL, PANEL)
        total = dot(src[h, :, pl.ds(at, width)], diag[h, pl.ds(at, PANEL), :], 1, 1)
        for d in range(1, reach):
            there = pl.ds(pl.multiple_of(lax.rem(j + panels - d, panels) * PANEL, PANEL), PANEL)
            total += dot(src[h, :, there], diag[h, there, d * PANEL : (d + 1) * PANEL], 1, 0)
        return total

    def across(src, h, b):
        if h == 1:
            return dot(src[0, :, :half], side[b], 1, 0)
        here = slice(b * part, (b + 1) * part)
        return sum(dot(src[1, :, e * part : (e + 1) * part], side[e, here, :], 1, 1) for e in range(2))

    for copy in diag_copies:
        copy.wait()
    for h in range(2):
        xe[h, :, half:] = xe[h, :, : width - PANEL]

    @pl.loop(0, panels)
    def _(j):
        here = pl.ds(pl.multiple_of(j * PANEL, PANEL), PANEL)
        for h in range(2):
            yf[h, :, here] = around(xe, h, j)

    for copy in side_copies:
        copy.wait()
    for h in range(2):
        for b in range(2):
            here = slice(b * part, (b + 1) * part)
            total = yf[h, :, here] + across(xe, h, b)
            ye[h, :, here] = total.astype(BF16)
            yf[h, :, here] = coef_linear * xe[h, :, here].astype(F32) + coef_cubic * total
    for h in range(2):
        ye[h, :, half:] = ye[h, :, : width - PANEL]

    for h in range(2):
        for b in range(2):
            here = slice(b * part, (b + 1) * part)
            yf[h, :, here] += coef_quintic * across(ye, h, b)

    @pl.loop(0, panels)
    def _(j):
        here = pl.ds(pl.multiple_of(j * PANEL, PANEL), PANEL)
        for h in range(2):
            out[h, :, here] = (yf[h, :, here] + coef_quintic * around(ye, h, j)).astype(BF16)

    last = [
        pltpu.make_async_copy(out.at[core], keep_ref.at[mine, :], sems.at[0]),
        pltpu.make_async_copy(out.at[1 - core], send_ref, sems.at[1]),
    ]
    for copy in last:
        copy.start()
    for copy in last:
        copy.wait()


def finish(core, own, other, starts, mine, theirs, panels, reach):
    rows, half = own.shape
    share = rows // 2
    part = half // 2
    width = reach * PANEL
    pieces = tuple(len(p) for p in mine)
    operands = [own, other, *mine[0], *mine[1], *theirs[0], *theirs[1]]
    place = jnp.stack([core, *starts]).astype(jnp.int32)
    anywhere = pl.BlockSpec(memory_space=pl.ANY)
    return pl.pallas_call(
        functools.partial(finish_kernel, panels, reach, part, pieces),
        out_shape=[jax.ShapeDtypeStruct((n, half), BF16) for n in (rows, share)],
        in_specs=[pl.BlockSpec(memory_space=pltpu.SMEM)] + [anywhere] * len(operands),
        out_specs=[anywhere] * 2,
        scratch_shapes=[
            pltpu.VMEM((2, share, half + width - PANEL), BF16),
            pltpu.VMEM((2, share, half + width - PANEL), BF16),
            pltpu.VMEM((2, share, half), F32),
            pltpu.VMEM((2, half, width), BF16),
            pltpu.VMEM((2, half, part), BF16),
            pltpu.VMEM((2, share, half), BF16),
            pltpu.SemaphoreType.DMA((len(operands),)),
        ],
        compiler_params=pltpu.CompilerParams(vmem_limit_bytes=56 * 2**20),
        cost_estimate=pl.CostEstimate(flops=16 * share * half * half, bytes_accessed=8 * half * half, transcendentals=0),
    )(place, *operands)


def add_kernel(kind, place_ref, forth_ref, back_ref, block_ref, *refs):
    out_refs, (own, sems) = refs[-4:-2] if kind != "last" else refs[-3:-2], refs[-2:]
    size = out_refs[0].shape[0]
    middle = size // 2
    copies = []
    for i in range(len(out_refs)):
        start = pl.multiple_of(place_ref[i], 16)
        copies.append(pltpu.make_async_copy(block_ref.at[pl.ds(start, size), :], own.at[i], sems.at[i]))
    for copy in copies:
        copy.start()
    for copy in copies:
        copy.wait()

    if kind == "last":
        total = own[0].astype(F32) + forth_ref[...].astype(F32) + back_ref[...].astype(F32)
        out_refs[0][...] = total.astype(BF16)
    elif kind == "middle":
        out_refs[0][...] = own[0] + forth_ref[...]
        out_refs[1][...] = own[1] + back_ref[...]
    else:
        out_refs[0][:middle] = own[0, :middle] + forth_ref[...]
        out_refs[0][middle:] = own[0, middle:]
        out_refs[1][:middle] = own[1, :middle]
        out_refs[1][middle:] = own[1, middle:] + back_ref[...]


def add_step(kind, size, starts, forth, back, block, after):
    outs = 1 if kind == "last" else 2
    cols = block.shape[1]
    vmem = pl.BlockSpec(memory_space=pltpu.VMEM)
    anywhere = pl.BlockSpec(memory_space=pl.ANY)
    return pl.pallas_call(
        functools.partial(add_kernel, kind),
        out_shape=[jax.ShapeDtypeStruct((size, cols), BF16)] * outs,
        in_specs=[pl.BlockSpec(memory_space=pltpu.SMEM), vmem, vmem] + [anywhere] * (1 + len(after)),
        out_specs=[vmem] * outs,
        scratch_shapes=[pltpu.VMEM((outs, size, cols), BF16), pltpu.SemaphoreType.DMA((outs,))],
        compiler_params=pltpu.CompilerParams(vmem_limit_bytes=8 * 2**20),
        cost_estimate=pl.CostEstimate(flops=STEP_FLOPS, bytes_accessed=8 * size * cols, transcendentals=0),
    )(jnp.stack(starts).astype(jnp.int32), forth, back, block, *after)


def gate(values, after):
    anywhere = pl.BlockSpec(memory_space=pl.ANY)
    return pl.pallas_call(
        lambda *refs: None,
        out_shape=[jax.ShapeDtypeStruct(v.shape, v.dtype) for v in values],
        in_specs=[anywhere] * (len(values) + len(after)),
        out_specs=[anywhere] * len(values),
        input_output_aliases={i: i for i in range(len(values))},
        compiler_params=pltpu.CompilerParams(vmem_limit_bytes=2**20),
        cost_estimate=pl.CostEstimate(flops=STEP_FLOPS, bytes_accessed=STEP_BYTES, transcendentals=0),
    )(*values, *after)


def ring_exchange(half, makers):
    count = lax.axis_size("row")
    order = list(range(0, count, 2)) + list(range(1, count, 2))[::-1]
    row = lax.axis_index("row")
    place = jnp.where(row % 2 == 0, row // 2, count - 1 - row // 2)
    far = count // 2
    turns = (1, -1)
    pairs = {t: [(order[p], order[(p + t) % count]) for p in range(count)] for t in turns}
    size = half // count
    parts = range(len(makers))

    def row_of(distance):
        return lax.rem(place + distance + count, count) * size

    def half_of(value, turn):
        middle = value.shape[0] // 2
        return value[:middle] if turn == 1 else value[middle:]

    def pass_on(values):
        values = lax.optimization_barrier(tuple(values))
        return [lax.ppermute(v, "row", pairs[t]) for t, v in zip(turns, values, strict=True)]

    blocks, held = [], []
    for make in makers:
        block, *chunk = make(row_of(far), size)
        blocks.append(block)
        held.append(chunk)
    after = blocks[1:]
    for distance in range(far - 1, -1, -1):
        kind = "last" if distance == 0 else "first" if distance == far - 1 else "middle"
        for k in parts:
            forth, back = pass_on(held[k])
            starts = [row_of(distance), row_of(-distance)][: 1 if distance == 0 else 2]
            held[k] = add_step(kind, size, starts, forth, back, blocks[k], after)
            after = [held[k][0]]
    pieces = [[held[k][0]] for k in parts]
    starts = [[row_of(0)] for k in parts]
    held = [[h[0], h[0]] for h in held]
    for distance in range(1, far + 1):
        for k in parts:
            if distance == far:
                held[k] = [half_of(h, t) for t, h in zip(turns, held[k], strict=True)]
            held[k] = gate(pass_on(held[k]), after)
            after = [held[k][0]]
            pieces[k] += held[k]
            ends = [row_of(-distance), row_of(distance)]
            if distance == far:
                ends[1] = ends[1] + size // 2
            starts[k] += ends
    return pieces, starts[0] + starts[1]


def plain_exchange(half, makers):
    pieces = []
    for make in makers:
        (block,) = make(jnp.int32(0), None)
        mine = lax.psum_scatter(block, "row", scatter_dimension=0, tiled=True)
        pieces.append([lax.all_gather(mine, "row", axis=0, tiled=True)])
    return pieces, [jnp.int32(0)] * len(makers)


def body(iterate):
    half = iterate.shape[1]
    count = lax.axis_size("row")
    core = lax.axis_index("col")
    panels = half // PANEL
    reach = (panels + 1) // 2
    swap = [(0, 1), (1, 0)]

    other = lax.ppermute(iterate, "col", swap)
    makers = [
        lambda start, size: diag_gram(iterate, reach * PANEL, start, size),
        lambda start, size: side_gram(core, iterate, other, start, size),
    ]
    exchange = ring_exchange if count <= RING_MOST else plain_exchange
    mine, starts = exchange(half, makers)
    theirs = [[lax.ppermute(piece, "col", swap) for piece in kind] for kind in mine]
    keep, send = finish(core, iterate, other, starts, mine, theirs, panels, reach)
    got = lax.ppermute(send, "col", swap)
    return lax.dynamic_update_slice_in_dim(keep, got, (1 - core) * got.shape[0], 0)


def solution(mesh):
    return jax.shard_map(
        body,
        mesh=mesh,
        in_specs=(P(("groups", "row"), "col"),),
        out_specs=P(("groups", "row"), "col"),
        check_vma=False,
    )
```

profile of v0, /device:TPU:0, one launch (start us, length us, event | category | flops | bytes accessed | tf_op | source)
XLA Modules:
  0.0 204.2 jit_solution(16703892632895407509)
XLA Ops:
  2.5 4.0 %shard_map.17 = (bf16[1792,1024]{1,0:T(8,128)(2,1)S(1)}, bf16[112,1024]{1,0:T(8,128)(2,1)S(1)}, bf16[112,1024]{1,0:T(8,128)(2,1)S(1)}) custom-call(s32[1]{0:T(128)} %bitcast.10.place_ref, bf16[1024,1792]{1,0:T(8,128)(2,1)S(1)} %copy-done.4), custom_call_target="tpu_custom_call" | custom-call | flops 3758096384 | bytes 7340032 | tf_op jit(solution)/shard_map/pallas_call | solution.py:54
  8.4 2.6 %collective-permute-start.1 = (bf16[112,1024]{1,0:T(8,128)(2,1)S(1)}, bf16[112,1024]{1,0:T(8,128)(2,1)S(1)}, u32[]{:S(2)}, u32[]{:S(2)}) collective-permute-start(bf16[112,1024]{1,0:T(8,128)(2,1)S(1)} %get-tuple-element.69), channel_id=1, source_target_pairs={{0,4},{4,8},{8,12},{12,14},{14,10},{10,6},{6,2},{2,0},{1,5},{5,9},... | collective-permute-start | bytes 688136 | tf_op jit(solution)/shard_map/ppermute | solution.py:293
  13.3 6.2 %shard_map.18 = (bf16[1792,896]{1,0:T(8,128)(2,1)S(1)}, bf16[112,896]{1,0:T(8,128)(2,1)S(1)}, bf16[112,896]{1,0:T(8,128)(2,1)S(1)}) custom-call(s32[2]{0:T(128)S(1)} %pad_add_fusion.3.place_ref, bf16[1024,1792]{1,0:T(8,128)(2,1)S(1)} %copy-done.5, bf16[1024,1792]{1,0:T(8,128)(2,1)} %collective-permute-done.other_ref.refs_1_), custom_call_target="tpu_custom_call" | custom-call | flops 8000000000 | bytes 11010048 | tf_op jit(solution)/shard_map/pallas_call | solution.py:90
  24.9 2.5 %collective-permute-done.5.forth_ref = bf16[112,896]{1,0:T(8,128)(2,1)S(1)} collective-permute-done((bf16[112,896]{1,0:T(8,128)(2,1)S(1)}, bf16[112,896]{1,0:T(8,128)(2,1)S(1)}, u32[]{:S(2)}, u32[]{:S(2)}) %collective-permute-start.5) | collective-permute-done | bytes 200736 | tf_op jit(solution)/shard_map/ppermute | solution.py:293
  27.4 2.1 %collective-permute-done.6.back_ref = bf16[112,896]{1,0:T(8,128)(2,1)S(1)} collective-permute-done((bf16[112,896]{1,0:T(8,128)(2,1)S(1)}, bf16[112,896]{1,0:T(8,128)(2,1)S(1)}, u32[]{:S(2)}, u32[]{:S(2)}) %collective-permute-start.6) | collective-permute-done | bytes 200736 | tf_op jit(solution)/shard_map/ppermute | solution.py:293
  32.6 4.6 %collective-permute-done.3.forth_ref = bf16[224,1024]{1,0:T(8,128)(2,1)S(1)} collective-permute-done((bf16[224,1024]{1,0:T(8,128)(2,1)S(1)}, bf16[224,1024]{1,0:T(8,128)(2,1)S(1)}, u32[]{:S(2)}, u32[]{:S(2)}) %collective-permute-start.3) | collective-permute-done | bytes 458784 | tf_op jit(solution)/shard_map/ppermute | solution.py:293
  42.6 3.2 %collective-permute-done.9.forth_ref = bf16[224,896]{1,0:T(8,128)(2,1)S(1)} collective-permute-done((bf16[224,896]{1,0:T(8,128)(2,1)S(1)}, bf16[224,896]{1,0:T(8,128)(2,1)S(1)}, u32[]{:S(2)}, u32[]{:S(2)}) %collective-permute-start.9) | collective-permute-done | bytes 401440 | tf_op jit(solution)/shard_map/ppermute | solution.py:293
  45.8 2.1 %collective-permute-done.10.back_ref = bf16[224,896]{1,0:T(8,128)(2,1)S(1)} collective-permute-done((bf16[224,896]{1,0:T(8,128)(2,1)S(1)}, bf16[224,896]{1,0:T(8,128)(2,1)S(1)}, u32[]{:S(2)}, u32[]{:S(2)}) %collective-permute-start.10) | collective-permute-done | bytes 401440 | tf_op jit(solution)/shard_map/ppermute | solution.py:293
  51.1 4.6 %collective-permute-done.7.forth_ref = bf16[224,1024]{1,0:T(8,128)(2,1)S(1)} collective-permute-done((bf16[224,1024]{1,0:T(8,128)(2,1)S(1)}, bf16[224,1024]{1,0:T(8,128)(2,1)S(1)}, u32[]{:S(2)}, u32[]{:S(2)}) %collective-permute-start.7) | collective-permute-done | bytes 458784 | tf_op jit(solution)/shard_map/ppermute | solution.py:293
  61.1 3.2 %collective-permute-done.13.forth_ref = bf16[224,896]{1,0:T(8,128)(2,1)S(1)} collective-permute-done((bf16[224,896]{1,0:T(8,128)(2,1)S(1)}, bf16[224,896]{1,0:T(8,128)(2,1)S(1)}, u32[]{:S(2)}, u32[]{:S(2)}) %collective-permute-start.13) | collective-permute-done | bytes 401440 | tf_op jit(solution)/shard_map/ppermute | solution.py:293
  64.3 2.1 %collective-permute-done.14.back_ref = bf16[224,896]{1,0:T(8,128)(2,1)S(1)} collective-permute-done((bf16[224,896]{1,0:T(8,128)(2,1)S(1)}, bf16[224,896]{1,0:T(8,128)(2,1)S(1)}, u32[]{:S(2)}, u32[]{:S(2)}) %collective-permute-start.14) | collective-permute-done | bytes 401440 | tf_op jit(solution)/shard_map/ppermute | solution.py:293
  69.5 4.6 %collective-permute-done.11.forth_ref = bf16[224,1024]{1,0:T(8,128)(2,1)S(1)} collective-permute-done((bf16[224,1024]{1,0:T(8,128)(2,1)S(1)}, bf16[224,1024]{1,0:T(8,128)(2,1)S(1)}, u32[]{:S(2)}, u32[]{:S(2)}) %collective-permute-start.11) | collective-permute-done | bytes 458784 | tf_op jit(solution)/shard_map/ppermute | solution.py:293
  78.8 3.9 %collective-permute-done.17.forth_ref = bf16[224,896]{1,0:T(8,128)(2,1)S(1)} collective-permute-done((bf16[224,896]{1,0:T(8,128)(2,1)S(1)}, bf16[224,896]{1,0:T(8,128)(2,1)S(1)}, u32[]{:S(2)}, u32[]{:S(2)}) %collective-permute-start.17) | collective-permute-done | bytes 401440 | tf_op jit(solution)/shard_map/ppermute | solution.py:293
  82.7 2.1 %collective-permute-done.18.back_ref = bf16[224,896]{1,0:T(8,128)(2,1)S(1)} collective-permute-done((bf16[224,896]{1,0:T(8,128)(2,1)S(1)}, bf16[224,896]{1,0:T(8,128)(2,1)S(1)}, u32[]{:S(2)}, u32[]{:S(2)}) %collective-permute-start.18) | collective-permute-done | bytes 401440 | tf_op jit(solution)/shard_map/ppermute | solution.py:293
  86.9 5.6 %collective-permute-done.15.refs_0_ = bf16[224,1024]{1,0:T(8,128)(2,1)S(1)} collective-permute-done((bf16[224,1024]{1,0:T(8,128)(2,1)S(1)}, bf16[224,1024]{1,0:T(8,128)(2,1)S(1)}, u32[]{:S(2)}, u32[]{:S(2)}) %collective-permute-start.15) | collective-permute-done | bytes 458784 | tf_op jit(solution)/shard_map/ppermute | solution.py:293
  94.9 6.2 %collective-permute-done.21.refs_0_ = bf16[224,896]{1,0:T(8,128)(2,1)S(1)} collective-permute-done((bf16[224,896]{1,0:T(8,128)(2,1)S(1)}, bf16[224,896]{1,0:T(8,128)(2,1)S(1)}, u32[]{:S(2)}, u32[]{:S(2)}) %collective-permute-start.21) | collective-permute-done | bytes 401440 | tf_op jit(solution)/shard_map/ppermute | solution.py:293
  103.9 7.1 %collective-permute-done.19.refs_0_ = bf16[224,1024]{1,0:T(8,128)(2,1)S(1)} collective-permute-done((bf16[224,1024]{1,0:T(8,128)(2,1)S(1)}, bf16[224,1024]{1,0:T(8,128)(2,1)S(1)}, u32[]{:S(2)}, u32[]{:S(2)}) %collective-permute-start.19) | collective-permute-done | bytes 458784 | tf_op jit(solution)/shard_map/ppermute | solution.py:293
  113.0 5.9 %collective-permute-done.25.refs_0_ = bf16[224,896]{1,0:T(8,128)(2,1)S(1)} collective-permute-done((bf16[224,896]{1,0:T(8,128)(2,1)S(1)}, bf16[224,896]{1,0:T(8,128)(2,1)S(1)}, u32[]{:S(2)}, u32[]{:S(2)}) %collective-permute-start.25) | collective-permute-done | bytes 401440 | tf_op jit(solution)/shard_map/ppermute | solution.py:293
  122.2 8.5 %collective-permute-done.23.refs_0_ = bf16[224,1024]{1,0:T(8,128)(2,1)S(1)} collective-permute-done((bf16[224,1024]{1,0:T(8,128)(2,1)S(1)}, bf16[224,1024]{1,0:T(8,128)(2,1)S(1)}, u32[]{:S(2)}, u32[]{:S(2)}) %collective-permute-start.23) | collective-permute-done | bytes 458784 | tf_op jit(solution)/shard_map/ppermute | solution.py:293
  134.4 6.0 %collective-permute-done.29.refs_0_ = bf16[224,896]{1,0:T(8,128)(2,1)S(1)} collective-permute-done((bf16[224,896]{1,0:T(8,128)(2,1)S(1)}, bf16[224,896]{1,0:T(8,128)(2,1)S(1)}, u32[]{:S(2)}, u32[]{:S(2)}) %collective-permute-start.29) | collective-permute-done | bytes 401440 | tf_op jit(solution)/shard_map/ppermute | solution.py:293
  143.3 3.2 %collective-permute-done.27.refs_0_ = bf16[112,1024]{1,0:T(8,128)(2,1)S(1)} collective-permute-done((bf16[112,1024]{1,0:T(8,128)(2,1)S(1)}, bf16[112,1024]{1,0:T(8,128)(2,1)S(1)}, u32[]{:S(2)}, u32[]{:S(2)}) %collective-permute-start.27) | collective-permute-done | bytes 229408 | tf_op jit(solution)/shard_map/ppermute | solution.py:293
  149.6 2.6 %collective-permute-done.31.refs_0_ = bf16[112,896]{1,0:T(8,128)(2,1)S(1)} collective-permute-done((bf16[112,896]{1,0:T(8,128)(2,1)S(1)}, bf16[112,896]{1,0:T(8,128)(2,1)S(1)}, u32[]{:S(2)}, u32[]{:S(2)}) %collective-permute-start.31) | collective-permute-done | bytes 200736 | tf_op jit(solution)/shard_map/ppermute | solution.py:293
  158.3 40.5 %shard_map.35 = (bf16[1024,1792]{1,0:T(8,128)(2,1)}, bf16[512,1792]{1,0:T(8,128)(2,1)}) custom-call(s32[19]{0:T(128)} %stack.40.place_ref, bf16[1024,1792]{1,0:T(8,128)(2,1)} %refs_0_.1, bf16[1024,1792]{1,0:T(8,128)(2,1)} %collective-permute-done.other_ref.refs_1_, bf16[224,1024]{1,0:T(8,128)(2,1)} %copy-done.6, bf16[224,1024]{1,0:T(8,128)(2,1)} %copy-done.7, ...), custom_call_target="tpu_custom_call" | custom-call | flops 26306674688 | bytes 25690112 | tf_op jit(solution)/shard_map/pallas_call | solution.py:199
  199.0 3.9 %collective-permute-done.51 = bf16[512,1792]{1,0:T(8,128)(2,1)S(1)} collective-permute-done((bf16[512,1792]{1,0:T(8,128)(2,1)}, bf16[512,1792]{1,0:T(8,128)(2,1)S(1)}, u32[]{:S(2)}, u32[]{:S(2)}) %collective-permute-start.51) | collective-permute-done | bytes 1835040 | tf_op jit(solution)/shard_map/ppermute | solution.py:351
  (185 shorter events, 66.5 us)
Async XLA Ops:
  8.4 13.3 %collective-permute-start.1 = (bf16[112,1024]{1,0:T(8,128)(2,1)S(1)}, bf16[112,1024]{1,0:T(8,128)(2,1)S(1)}, u32[]{:S(2)}, u32[]{:S(2)}) collective-permute-start(bf16[112,1024]{1,0:T(8,128)(2,1)S(1)} %get-tuple-element.69), channel_id=1, source_target_pairs={{0,4},{4,8},{8,12},{12,14},{14,10},{10,6},{6,2},{2,0},{1,5},{5,9},... | collective-permute-start | bytes 688136 | tf_op jit(solution)/shard_map/ppermute | solution.py:293
  22.8 14.4 %collective-permute-start.3 = (bf16[224,1024]{1,0:T(8,128)(2,1)S(1)}, bf16[224,1024]{1,0:T(8,128)(2,1)S(1)}, u32[]{:S(2)}, u32[]{:S(2)}) collective-permute-start(bf16[224,1024]{1,0:T(8,128)(2,1)S(1)} %get-tuple-element.79.refs_0_), channel_id=1, source_target_pairs={{0,4},{4,8},{8,12},{12,14},{14,10},{10,6},{6,2},{2,0},{1,5},{5,9},... | collective-permute-start | bytes 1376264 | tf_op jit(solution)/shard_map/ppermute | solution.py:293
  24.9 14.4 %collective-permute-start.4 = (bf16[224,1024]{1,0:T(8,128)(2,1)S(1)}, bf16[224,1024]{1,0:T(8,128)(2,1)S(1)}, u32[]{:S(2)}, u32[]{:S(2)}) collective-permute-start(bf16[224,1024]{1,0:T(8,128)(2,1)S(1)} %get-tuple-element.74), channel_id=1, source_target_pairs={{0,2},{4,0},{8,4},{12,8},{14,12},{10,14},{6,10},{2,6},{1,3},{5,1},... | collective-permute-start | bytes 1376264 | tf_op jit(solution)/shard_map/ppermute | solution.py:293
  30.5 15.3 %collective-permute-start.9 = (bf16[224,896]{1,0:T(8,128)(2,1)S(1)}, bf16[224,896]{1,0:T(8,128)(2,1)S(1)}, u32[]{:S(2)}, u32[]{:S(2)}) collective-permute-start(bf16[224,896]{1,0:T(8,128)(2,1)S(1)} %get-tuple-element.80.refs_0_), channel_id=1, source_target_pairs={{0,4},{4,8},{8,12},{12,14},{14,10},{10,6},{6,2},{2,0},{1,5},{5,9},... | collective-permute-start | bytes 1204232 | tf_op jit(solution)/shard_map/ppermute | solution.py:293
  32.2 15.8 %collective-permute-start.10 = (bf16[224,896]{1,0:T(8,128)(2,1)S(1)}, bf16[224,896]{1,0:T(8,128)(2,1)S(1)}, u32[]{:S(2)}, u32[]{:S(2)}) collective-permute-start(bf16[224,896]{1,0:T(8,128)(2,1)S(1)} %get-tuple-element.84), channel_id=1, source_target_pairs={{0,2},{4,0},{8,4},{12,8},{14,12},{10,14},{6,10},{2,6},{1,3},{5,1},... | collective-permute-start | bytes 1204232 | tf_op jit(solution)/shard_map/ppermute | solution.py:293
  40.5 15.1 %collective-permute-start.7 = (bf16[224,1024]{1,0:T(8,128)(2,1)S(1)}, bf16[224,1024]{1,0:T(8,128)(2,1)S(1)}, u32[]{:S(2)}, u32[]{:S(2)}) collective-permute-start(bf16[224,1024]{1,0:T(8,128)(2,1)S(1)} %get-tuple-element.85.refs_0_), channel_id=1, source_target_pairs={{0,4},{4,8},{8,12},{12,14},{14,10},{10,6},{6,2},{2,0},{1,5},{5,9},... | collective-permute-start | bytes 1376264 | tf_op jit(solution)/shard_map/ppermute | solution.py:293
  42.2 15.6 %collective-permute-start.8 = (bf16[224,1024]{1,0:T(8,128)(2,1)S(1)}, bf16[224,1024]{1,0:T(8,128)(2,1)S(1)}, u32[]{:S(2)}, u32[]{:S(2)}) collective-permute-start(bf16[224,1024]{1,0:T(8,128)(2,1)S(1)} %get-tuple-element.82), channel_id=1, source_target_pairs={{0,2},{4,0},{8,4},{12,8},{14,12},{10,14},{6,10},{2,6},{1,3},{5,1},... | collective-permute-start | bytes 1376264 | tf_op jit(solution)/shard_map/ppermute | solution.py:293
  49.0 15.2 %collective-permute-start.13 = (bf16[224,896]{1,0:T(8,128)(2,1)S(1)}, bf16[224,896]{1,0:T(8,128)(2,1)S(1)}, u32[]{:S(2)}, u32[]{:S(2)}) collective-permute-start(bf16[224,896]{1,0:T(8,128)(2,1)S(1)} %get-tuple-element.86.refs_0_), channel_id=1, source_target_pairs={{0,4},{4,8},{8,12},{12,14},{14,10},{10,6},{6,2},{2,0},{1,5},{5,9},... | collective-permute-start | bytes 1204232 | tf_op jit(solution)/shard_map/ppermute | solution.py:293
  50.7 15.7 %collective-permute-start.14 = (bf16[224,896]{1,0:T(8,128)(2,1)S(1)}, bf16[224,896]{1,0:T(8,128)(2,1)S(1)}, u32[]{:S(2)}, u32[]{:S(2)}) collective-permute-start(bf16[224,896]{1,0:T(8,128)(2,1)S(1)} %get-tuple-element.90), channel_id=1, source_target_pairs={{0,2},{4,0},{8,4},{12,8},{14,12},{10,14},{6,10},{2,6},{1,3},{5,1},... | collective-permute-start | bytes 1204232 | tf_op jit(solution)/shard_map/ppermute | solution.py:293
  59.0 15.1 %collective-permute-start.11 = (bf16[224,1024]{1,0:T(8,128)(2,1)S(1)}, bf16[224,1024]{1,0:T(8,128)(2,1)S(1)}, u32[]{:S(2)}, u32[]{:S(2)}) collective-permute-start(bf16[224,1024]{1,0:T(8,128)(2,1)S(1)} %get-tuple-element.91.refs_0_), channel_id=1, source_target_pairs={{0,4},{4,8},{8,12},{12,14},{14,10},{10,6},{6,2},{2,0},{1,5},{5,9},... | collective-permute-start | bytes 1376264 | tf_op jit(solution)/shard_map/ppermute | solution.py:293
  60.6 15.6 %collective-permute-start.12 = (bf16[224,1024]{1,0:T(8,128)(2,1)S(1)}, bf16[224,1024]{1,0:T(8,128)(2,1)S(1)}, u32[]{:S(2)}, u32[]{:S(2)}) collective-permute-start(bf16[224,1024]{1,0:T(8,128)(2,1)S(1)} %get-tuple-element.88), channel_id=1, source_target_pairs={{0,2},{4,0},{8,4},{12,8},{14,12},{10,14},{6,10},{2,6},{1,3},{5,1},... | collective-permute-start | bytes 1376264 | tf_op jit(solution)/shard_map/ppermute | solution.py:293
  67.4 15.3 %collective-permute-start.17 = (bf16[224,896]{1,0:T(8,128)(2,1)S(1)}, bf16[224,896]{1,0:T(8,128)(2,1)S(1)}, u32[]{:S(2)}, u32[]{:S(2)}) collective-permute-start(bf16[224,896]{1,0:T(8,128)(2,1)S(1)} %get-tuple-element.92.refs_0_), channel_id=1, source_target_pairs={{0,4},{4,8},{8,12},{12,14},{14,10},{10,6},{6,2},{2,0},{1,5},{5,9},... | collective-permute-start | bytes 1204232 | tf_op jit(solution)/shard_map/ppermute | solution.py:293
  69.1 15.7 %collective-permute-start.18 = (bf16[224,896]{1,0:T(8,128)(2,1)S(1)}, bf16[224,896]{1,0:T(8,128)(2,1)S(1)}, u32[]{:S(2)}, u32[]{:S(2)}) collective-permute-start(bf16[224,896]{1,0:T(8,128)(2,1)S(1)} %get-tuple-element.96), channel_id=1, source_target_pairs={{0,2},{4,0},{8,4},{12,8},{14,12},{10,14},{6,10},{2,6},{1,3},{5,1},... | collective-permute-start | bytes 1204232 | tf_op jit(solution)/shard_map/ppermute | solution.py:293
  76.7 56.2 %collective-permute-start.33 = (bf16[224,1024]{1,0:T(8,128)(2,1)S(1)}, bf16[224,1024]{1,0:T(8,128)(2,1)S(1)}, u32[]{:S(2)}, u32[]{:S(2)}) collective-permute-start(bf16[224,1024]{1,0:T(8,128)(2,1)S(1)} %shard_map.25.refs_0_.refs_2_), channel_id=1, source_target_pairs={{0,1},{1,0},{2,3},{3,2},{4,5},{5,4},{6,7},{7,6},{8,9},{9,8},{10,11... | collective-permute-start | bytes 1376264 | tf_op jit(solution)/shard_map/ppermute | solution.py:349
  76.7 15.8 %collective-permute-start.15 = (bf16[224,1024]{1,0:T(8,128)(2,1)S(1)}, bf16[224,1024]{1,0:T(8,128)(2,1)S(1)}, u32[]{:S(2)}, u32[]{:S(2)}) collective-permute-start(bf16[224,1024]{1,0:T(8,128)(2,1)S(1)} %shard_map.25.refs_0_.refs_2_), channel_id=1, source_target_pairs={{0,4},{4,8},{8,12},{12,14},{14,10},{10,6},{6,2},{2,0},{1,5},{5,9},... | collective-permute-start | bytes 1376264 | tf_op jit(solution)/shard_map/ppermute | solution.py:293
  78.4 16.1 %collective-permute-start.16 = (bf16[224,1024]{1,0:T(8,128)(2,1)S(1)}, bf16[224,1024]{1,0:T(8,128)(2,1)S(1)}, u32[]{:S(2)}, u32[]{:S(2)}) collective-permute-start(bf16[224,1024]{1,0:T(8,128)(2,1)S(1)} %shard_map.25.refs_0_.refs_2_), channel_id=1, source_target_pairs={{0,2},{4,0},{8,4},{12,8},{14,12},{10,14},{6,10},{2,6},{1,3},{5,1},... | collective-permute-start | bytes 1376264 | tf_op jit(solution)/shard_map/ppermute | solution.py:293
  85.2 47.6 %collective-permute-start.42 = (bf16[224,896]{1,0:T(8,128)(2,1)S(1)}, bf16[224,896]{1,0:T(8,128)(2,1)S(1)}, u32[]{:S(2)}, u32[]{:S(2)}) collective-permute-start(bf16[224,896]{1,0:T(8,128)(2,1)S(1)} %shard_map.26.refs_2_.refs_11_), channel_id=1, source_target_pairs={{0,1},{1,0},{2,3},{3,2},{4,5},{5,4},{6,7},{7,6},{8,9},{9,8},{10,11... | collective-permute-start | bytes 1204232 | tf_op jit(solution)/shard_map/ppermute | solution.py:349
  85.3 15.9 %collective-permute-start.21 = (bf16[224,896]{1,0:T(8,128)(2,1)S(1)}, bf16[224,896]{1,0:T(8,128)(2,1)S(1)}, u32[]{:S(2)}, u32[]{:S(2)}) collective-permute-start(bf16[224,896]{1,0:T(8,128)(2,1)S(1)} %shard_map.26.refs_2_.refs_11_), channel_id=1, source_target_pairs={{0,4},{4,8},{8,12},{12,14},{14,10},{10,6},{6,2},{2,0},{1,5},{5,9},... | collective-permute-start | bytes 1204232 | tf_op jit(solution)/shard_map/ppermute | solution.py:293
  94.5 16.4 %collective-permute-start.19 = (bf16[224,1024]{1,0:T(8,128)(2,1)S(1)}, bf16[224,1024]{1,0:T(8,128)(2,1)S(1)}, u32[]{:S(2)}, u32[]{:S(2)}) collective-permute-start(bf16[224,1024]{1,0:T(8,128)(2,1)S(1)} %get-tuple-element.97.refs_2_.refs_3_), channel_id=1, source_target_pairs={{0,4},{4,8},{8,12},{12,14},{14,10},{10,6},{6,2},{2,0},{1,5},{5,9},... | collective-permute-start | bytes 1376264 | tf_op jit(solution)/shard_map/ppermute | solution.py:293
  101.1 11.8 %collective-permute-start.20 = (bf16[224,1024]{1,0:T(8,128)(2,1)S(1)}, bf16[224,1024]{1,0:T(8,128)(2,1)S(1)}, u32[]{:S(2)}, u32[]{:S(2)}) collective-permute-start(bf16[224,1024]{1,0:T(8,128)(2,1)S(1)} %get-tuple-element.98.refs_4_), channel_id=1, source_target_pairs={{0,2},{4,0},{8,4},{12,8},{14,12},{10,14},{6,10},{2,6},{1,3},{5,1},... | collective-permute-start | bytes 1376264 | tf_op jit(solution)/shard_map/ppermute | solution.py:293
  103.1 15.7 %collective-permute-start.25 = (bf16[224,896]{1,0:T(8,128)(2,1)S(1)}, bf16[224,896]{1,0:T(8,128)(2,1)S(1)}, u32[]{:S(2)}, u32[]{:S(2)}) collective-permute-start(bf16[224,896]{1,0:T(8,128)(2,1)S(1)} %get-tuple-element.103.refs_2_.refs_12_), channel_id=1, source_target_pairs={{0,4},{4,8},{8,12},{12,14},{14,10},{10,6},{6,2},{2,0},{1,5},{5,9},... | collective-permute-start | bytes 1204232 | tf_op jit(solution)/shard_map/ppermute | solution.py:293
  113.0 20.5 %collective-permute-start.44 = (bf16[224,896]{1,0:T(8,128)(2,1)S(1)}, bf16[224,896]{1,0:T(8,128)(2,1)S(1)}, u32[]{:S(2)}, u32[]{:S(2)}) collective-permute-start(bf16[224,896]{1,0:T(8,128)(2,1)S(1)} %get-tuple-element.109), channel_id=1, source_target_pairs={{0,1},{1,0},{2,3},{3,2},{4,5},{5,4},{6,7},{7,6},{8,9},{9,8},{10,11... | collective-permute-start | bytes 1204232 | tf_op jit(solution)/shard_map/ppermute | solution.py:349
  118.9 11.8 %collective-permute-start.23 = (bf16[224,1024]{1,0:T(8,128)(2,1)S(1)}, bf16[224,1024]{1,0:T(8,128)(2,1)S(1)}, u32[]{:S(2)}, u32[]{:S(2)}) collective-permute-start(bf16[224,1024]{1,0:T(8,128)(2,1)S(1)} %get-tuple-element.104.refs_2_.refs_5_), channel_id=1, source_target_pairs={{0,4},{4,8},{8,12},{12,14},{14,10},{10,6},{6,2},{2,0},{1,5},{5,9},... | collective-permute-start | bytes 1376264 | tf_op jit(solution)/shard_map/ppermute | solution.py:293
  120.9 11.3 %collective-permute-start.24 = (bf16[224,1024]{1,0:T(8,128)(2,1)S(1)}, bf16[224,1024]{1,0:T(8,128)(2,1)S(1)}, u32[]{:S(2)}, u32[]{:S(2)}) collective-permute-start(bf16[224,1024]{1,0:T(8,128)(2,1)S(1)} %get-tuple-element.105.refs_6_), channel_id=1, source_target_pairs={{0,2},{4,0},{8,4},{12,8},{14,12},{10,14},{6,10},{2,6},{1,3},{5,1},... | collective-permute-start | bytes 1376264 | tf_op jit(solution)/shard_map/ppermute | solution.py:293
  (66 other events, 562.0 us)
where the time goes:
time: 204 us
  waiting for transfers between devices  93.8 us (46%)
  Pallas kernels  58.3 us (29%)
  starting transfers between devices  41.3 us (20%)
  local copies, waits for them, and re-layouts  9.89 us (5%)
    ppermute x32, waiting for transfers between devices, pass_on(): lax.ppermute(v, 'row', pairs[t])  88.3 us
    pallas_call x1, Pallas kernels, finish(): pl.pallas_call(functools.partial(finish_kernel, panels, reach, part, piec...  40.5 us
    ppermute x32, starting transfers between devices, pass_on(): lax.ppermute(v, 'row', pairs[t])  37.1 us
    unnamed x76, local copies, waits for them, and re-layouts  7.89 us
    pallas_call x8, Pallas kernels, add_step(): pl.pallas_call(functools.partial(add_kernel, kind), out_shape=[jax.ShapeD...  7.58 us
    pallas_call x1, Pallas kernels, side_gram(): pl.pallas_call(functools.partial(side_kernel, len(outs)), out_shape=outs,...  6.24 us
  transfers between devices with their start and end apart: 52, of which 28 were waited for; matrix products, arithmetic and copies ran while one was open for 0% of the time, Pallas kernels for 9%

commit v1 on v0

--- a/solution.py
+++ b/solution.py
@@ -16,7 +16,8 @@
 PANEL = 256
 RING_MOST = 16
 STEP_BYTES = 20 * 2**20
-STEP_FLOPS = 8 * 10**9
+SUM_FLOPS = 8 * 10**9
+GATE_FLOPS = 3 * 10**9
 F32 = jnp.float32
 BF16 = jnp.bfloat16
 
@@ -93,7 +94,7 @@
         in_specs=[pl.BlockSpec(memory_space=pltpu.SMEM), vmem, vmem],
         out_specs=[vmem] * len(outs),
         compiler_params=pltpu.CompilerParams(vmem_limit_bytes=40 * 2**20),
-        cost_estimate=pl.CostEstimate(flops=STEP_FLOPS, bytes_accessed=6 * rows * half, transcendentals=0),
+        cost_estimate=pl.CostEstimate(flops=SUM_FLOPS, bytes_accessed=6 * rows * half, transcendentals=0),
     )(jnp.stack([start, core]), own, other)
 
 
@@ -253,7 +254,7 @@
         out_specs=[vmem] * outs,
         scratch_shapes=[pltpu.VMEM((outs, size, cols), BF16), pltpu.SemaphoreType.DMA((outs,))],
         compiler_params=pltpu.CompilerParams(vmem_limit_bytes=8 * 2**20),
-        cost_estimate=pl.CostEstimate(flops=STEP_FLOPS, bytes_accessed=8 * size * cols, transcendentals=0),
+        cost_estimate=pl.CostEstimate(flops=SUM_FLOPS, bytes_accessed=8 * size * cols, transcendentals=0),
     )(jnp.stack(starts).astype(jnp.int32), forth, back, block, *after)
 
 
@@ -266,7 +267,7 @@
         out_specs=[anywhere] * len(values),
         input_output_aliases={i: i for i in range(len(values))},
         compiler_params=pltpu.CompilerParams(vmem_limit_bytes=2**20),
-        cost_estimate=pl.CostEstimate(flops=STEP_FLOPS, bytes_accessed=STEP_BYTES, transcendentals=0),
+        cost_estimate=pl.CostEstimate(flops=GATE_FLOPS, bytes_accessed=STEP_BYTES, transcendentals=0),
     )(*values, *after)
 
 

time: 204 us -> 202 us (level)
  waiting for transfers between devices: 93.8 us -> 91.1 us
    ppermute x32, waiting for transfers between devices: 88.3 us -> 85.7 us  [pass_on(): lax.ppermute(v, 'row', pairs[t])]
    unnamed x76 -> x78, local copies, waits for them, and re-layouts: 7.89 us -> 7.82 us
  transfers between devices with their start and end apart: 52 -> 52, of which waited for: 28 -> 29; matrix products, arithmetic and copies ran while one was open for 0% -> 1% of each run, Pallas kernels for 9% -> 9%
where the time goes in v1:
time: 202 us
  waiting for transfers between devices  91.1 us (45%)
  Pallas kernels  58.3 us (29%)
  starting transfers between devices  41.8 us (21%)
  local copies, waits for them, and re-layouts  9.92 us (5%)
    ppermute x32, waiting for transfers between devices, pass_on(): lax.ppermute(v, 'row', pairs[t])  85.7 us
    pallas_call x1, Pallas kernels, finish(): pl.pallas_call(functools.partial(finish_kernel, panels, reach, part, piec...  40.5 us
    ppermute x32, starting transfers between devices, pass_on(): lax.ppermute(v, 'row', pairs[t])  37.6 us
    unnamed x78, local copies, waits for them, and re-layouts  7.82 us
    pallas_call x8, Pallas kernels, add_step(): pl.pallas_call(functools.partial(add_kernel, kind), out_shape=[jax.ShapeD...  7.56 us
    pallas_call x1, Pallas kernels, side_gram(): pl.pallas_call(functools.partial(side_kernel, len(outs)), out_shape=outs,...  6.24 us
  transfers between devices with their start and end apart: 52, of which 29 were waited for; matrix products, arithmetic and copies ran while one was open for 1% of the time, Pallas kernels for 9%

profile of v1, /device:TPU:0, one launch (start us, length us, event | category | flops | bytes accessed | tf_op | source)
XLA Modules:
  0.0 201.9 jit_solution(17149555088528020618)
XLA Ops:
  2.5 4.0 %shard_map.17 = (bf16[1792,1024]{1,0:T(8,128)(2,1)S(1)}, bf16[112,1024]{1,0:T(8,128)(2,1)S(1)}, bf16[112,1024]{1,0:T(8,128)(2,1)S(1)}) custom-call(s32[1]{0:T(128)} %bitcast.10.place_ref, bf16[1024,1792]{1,0:T(8,128)(2,1)S(1)} %copy-done.4), custom_call_target="tpu_custom_call" | custom-call | flops 3758096384 | bytes 7340032 | tf_op jit(solution)/shard_map/pallas_call | solution.py:55
  8.4 2.6 %collective-permute-start.1 = (bf16[112,1024]{1,0:T(8,128)(2,1)S(1)}, bf16[112,1024]{1,0:T(8,128)(2,1)S(1)}, u32[]{:S(2)}, u32[]{:S(2)}) collective-permute-start(bf16[112,1024]{1,0:T(8,128)(2,1)S(1)} %get-tuple-element.69), channel_id=1, source_target_pairs={{0,4},{4,8},{8,12},{12,14},{14,10},{10,6},{6,2},{2,0},{1,5},{5,9},... | collective-permute-start | bytes 688136 | tf_op jit(solution)/shard_map/ppermute | solution.py:294
  13.3 6.2 %shard_map.18 = (bf16[1792,896]{1,0:T(8,128)(2,1)S(1)}, bf16[112,896]{1,0:T(8,128)(2,1)S(1)}, bf16[112,896]{1,0:T(8,128)(2,1)S(1)}) custom-call(s32[2]{0:T(128)S(1)} %pad_add_fusion.3.place_ref, bf16[1024,1792]{1,0:T(8,128)(2,1)S(1)} %copy-done.5, bf16[1024,1792]{1,0:T(8,128)(2,1)} %collective-permute-done.other_ref.refs_1_), custom_call_target="tpu_custom_call" | custom-call | flops 8000000000 | bytes 11010048 | tf_op jit(solution)/shard_map/pallas_call | solution.py:91
  24.9 2.5 %collective-permute-done.5.forth_ref = bf16[112,896]{1,0:T(8,128)(2,1)S(1)} collective-permute-done((bf16[112,896]{1,0:T(8,128)(2,1)S(1)}, bf16[112,896]{1,0:T(8,128)(2,1)S(1)}, u32[]{:S(2)}, u32[]{:S(2)}) %collective-permute-start.5) | collective-permute-done | bytes 200736 | tf_op jit(solution)/shard_map/ppermute | solution.py:294
  27.4 2.1 %collective-permute-done.6.back_ref = bf16[112,896]{1,0:T(8,128)(2,1)S(1)} collective-permute-done((bf16[112,896]{1,0:T(8,128)(2,1)S(1)}, bf16[112,896]{1,0:T(8,128)(2,1)S(1)}, u32[]{:S(2)}, u32[]{:S(2)}) %collective-permute-start.6) | collective-permute-done | bytes 200736 | tf_op jit(solution)/shard_map/ppermute | solution.py:294
  32.6 4.6 %collective-permute-done.3.forth_ref = bf16[224,1024]{1,0:T(8,128)(2,1)S(1)} collective-permute-done((bf16[224,1024]{1,0:T(8,128)(2,1)S(1)}, bf16[224,1024]{1,0:T(8,128)(2,1)S(1)}, u32[]{:S(2)}, u32[]{:S(2)}) %collective-permute-start.3) | collective-permute-done | bytes 458784 | tf_op jit(solution)/shard_map/ppermute | solution.py:294
  37.2 2.1 %collective-permute-done.4.back_ref = bf16[224,1024]{1,0:T(8,128)(2,1)S(1)} collective-permute-done((bf16[224,1024]{1,0:T(8,128)(2,1)S(1)}, bf16[224,1024]{1,0:T(8,128)(2,1)S(1)}, u32[]{:S(2)}, u32[]{:S(2)}) %collective-permute-start.4) | collective-permute-done | bytes 458784 | tf_op jit(solution)/shard_map/ppermute | solution.py:294
  42.6 3.2 %collective-permute-done.9.forth_ref = bf16[224,896]{1,0:T(8,128)(2,1)S(1)} collective-permute-done((bf16[224,896]{1,0:T(8,128)(2,1)S(1)}, bf16[224,896]{1,0:T(8,128)(2,1)S(1)}, u32[]{:S(2)}, u32[]{:S(2)}) %collective-permute-start.9) | collective-permute-done | bytes 401440 | tf_op jit(solution)/shard_map/ppermute | solution.py:294
  51.1 4.6 %collective-permute-done.7.forth_ref = bf16[224,1024]{1,0:T(8,128)(2,1)S(1)} collective-permute-done((bf16[224,1024]{1,0:T(8,128)(2,1)S(1)}, bf16[224,1024]{1,0:T(8,128)(2,1)S(1)}, u32[]{:S(2)}, u32[]{:S(2)}) %collective-permute-start.7) | collective-permute-done | bytes 458784 | tf_op jit(solution)/shard_map/ppermute | solution.py:294
  61.1 3.2 %collective-permute-done.13.forth_ref = bf16[224,896]{1,0:T(8,128)(2,1)S(1)} collective-permute-done((bf16[224,896]{1,0:T(8,128)(2,1)S(1)}, bf16[224,896]{1,0:T(8,128)(2,1)S(1)}, u32[]{:S(2)}, u32[]{:S(2)}) %collective-permute-start.13) | collective-permute-done | bytes 401440 | tf_op jit(solution)/shard_map/ppermute | solution.py:294
  69.5 4.6 %collective-permute-done.11.forth_ref = bf16[224,1024]{1,0:T(8,128)(2,1)S(1)} collective-permute-done((bf16[224,1024]{1,0:T(8,128)(2,1)S(1)}, bf16[224,1024]{1,0:T(8,128)(2,1)S(1)}, u32[]{:S(2)}, u32[]{:S(2)}) %collective-permute-start.11) | collective-permute-done | bytes 458784 | tf_op jit(solution)/shard_map/ppermute | solution.py:294
  74.1 2.1 %collective-permute-done.12.back_ref = bf16[224,1024]{1,0:T(8,128)(2,1)S(1)} collective-permute-done((bf16[224,1024]{1,0:T(8,128)(2,1)S(1)}, bf16[224,1024]{1,0:T(8,128)(2,1)S(1)}, u32[]{:S(2)}, u32[]{:S(2)}) %collective-permute-start.12) | collective-permute-done | bytes 458784 | tf_op jit(solution)/shard_map/ppermute | solution.py:294
  78.7 4.0 %collective-permute-done.17.forth_ref = bf16[224,896]{1,0:T(8,128)(2,1)S(1)} collective-permute-done((bf16[224,896]{1,0:T(8,128)(2,1)S(1)}, bf16[224,896]{1,0:T(8,128)(2,1)S(1)}, u32[]{:S(2)}, u32[]{:S(2)}) %collective-permute-start.17) | collective-permute-done | bytes 401440 | tf_op jit(solution)/shard_map/ppermute | solution.py:294
  87.2 5.3 %collective-permute-done.15.refs_0_ = bf16[224,1024]{1,0:T(8,128)(2,1)S(1)} collective-permute-done((bf16[224,1024]{1,0:T(8,128)(2,1)S(1)}, bf16[224,1024]{1,0:T(8,128)(2,1)S(1)}, u32[]{:S(2)}, u32[]{:S(2)}) %collective-permute-start.15) | collective-permute-done | bytes 458784 | tf_op jit(solution)/shard_map/ppermute | solution.py:294
  92.5 2.1 %collective-permute-done.16.refs_1_ = bf16[224,1024]{1,0:T(8,128)(2,1)S(1)} collective-permute-done((bf16[224,1024]{1,0:T(8,128)(2,1)S(1)}, bf16[224,1024]{1,0:T(8,128)(2,1)S(1)}, u32[]{:S(2)}, u32[]{:S(2)}) %collective-permute-start.16) | collective-permute-done | bytes 458784 | tf_op jit(solution)/shard_map/ppermute | solution.py:294
  96.7 4.5 %collective-permute-done.21.refs_0_ = bf16[224,896]{1,0:T(8,128)(2,1)S(1)} collective-permute-done((bf16[224,896]{1,0:T(8,128)(2,1)S(1)}, bf16[224,896]{1,0:T(8,128)(2,1)S(1)}, u32[]{:S(2)}, u32[]{:S(2)}) %collective-permute-start.21) | collective-permute-done | bytes 401440 | tf_op jit(solution)/shard_map/ppermute | solution.py:294
  104.8 6.1 %collective-permute-done.19.refs_0_ = bf16[224,1024]{1,0:T(8,128)(2,1)S(1)} collective-permute-done((bf16[224,1024]{1,0:T(8,128)(2,1)S(1)}, bf16[224,1024]{1,0:T(8,128)(2,1)S(1)}, u32[]{:S(2)}, u32[]{:S(2)}) %collective-permute-start.19) | collective-permute-done | bytes 458784 | tf_op jit(solution)/shard_map/ppermute | solution.py:294
  113.7 5.9 %collective-permute-done.25.refs_0_ = bf16[224,896]{1,0:T(8,128)(2,1)S(1)} collective-permute-done((bf16[224,896]{1,0:T(8,128)(2,1)S(1)}, bf16[224,896]{1,0:T(8,128)(2,1)S(1)}, u32[]{:S(2)}, u32[]{:S(2)}) %collective-permute-start.25) | collective-permute-done | bytes 401440 | tf_op jit(solution)/shard_map/ppermute | solution.py:294
  123.1 6.3 %collective-permute-done.23.refs_0_ = bf16[224,1024]{1,0:T(8,128)(2,1)S(1)} collective-permute-done((bf16[224,1024]{1,0:T(8,128)(2,1)S(1)}, bf16[224,1024]{1,0:T(8,128)(2,1)S(1)}, u32[]{:S(2)}, u32[]{:S(2)}) %collective-permute-start.23) | collective-permute-done | bytes 458784 | tf_op jit(solution)/shard_map/ppermute | solution.py:294
  132.9 4.5 %collective-permute-done.29.refs_0_ = bf16[224,896]{1,0:T(8,128)(2,1)S(1)} collective-permute-done((bf16[224,896]{1,0:T(8,128)(2,1)S(1)}, bf16[224,896]{1,0:T(8,128)(2,1)S(1)}, u32[]{:S(2)}, u32[]{:S(2)}) %collective-permute-start.29) | collective-permute-done | bytes 401440 | tf_op jit(solution)/shard_map/ppermute | solution.py:294
  140.8 3.4 %collective-permute-done.27.refs_0_ = bf16[112,1024]{1,0:T(8,128)(2,1)S(1)} collective-permute-done((bf16[112,1024]{1,0:T(8,128)(2,1)S(1)}, bf16[112,1024]{1,0:T(8,128)(2,1)S(1)}, u32[]{:S(2)}, u32[]{:S(2)}) %collective-permute-start.27) | collective-permute-done | bytes 229408 | tf_op jit(solution)/shard_map/ppermute | solution.py:294
  147.4 2.6 %collective-permute-done.31.refs_0_ = bf16[112,896]{1,0:T(8,128)(2,1)S(1)} collective-permute-done((bf16[112,896]{1,0:T(8,128)(2,1)S(1)}, bf16[112,896]{1,0:T(8,128)(2,1)S(1)}, u32[]{:S(2)}, u32[]{:S(2)}) %collective-permute-start.31) | collective-permute-done | bytes 200736 | tf_op jit(solution)/shard_map/ppermute | solution.py:294
  156.0 40.5 %shard_map.35 = (bf16[1024,1792]{1,0:T(8,128)(2,1)}, bf16[512,1792]{1,0:T(8,128)(2,1)}) custom-call(s32[19]{0:T(128)} %stack.40.place_ref, bf16[1024,1792]{1,0:T(8,128)(2,1)} %refs_0_.1, bf16[1024,1792]{1,0:T(8,128)(2,1)} %collective-permute-done.other_ref.refs_1_, bf16[224,1024]{1,0:T(8,128)(2,1)} %copy-done.6, bf16[224,1024]{1,0:T(8,128)(2,1)} %copy-done.9, ...), custom_call_target="tpu_custom_call" | custom-call | flops 26306674688 | bytes 25690112 | tf_op jit(solution)/shard_map/pallas_call | solution.py:200
  196.7 3.9 %collective-permute-done.51 = bf16[512,1792]{1,0:T(8,128)(2,1)S(1)} collective-permute-done((bf16[512,1792]{1,0:T(8,128)(2,1)}, bf16[512,1792]{1,0:T(8,128)(2,1)S(1)}, u32[]{:S(2)}, u32[]{:S(2)}) %collective-permute-start.51) | collective-permute-done | bytes 1835040 | tf_op jit(solution)/shard_map/ppermute | solution.py:352
  (187 shorter events, 70.7 us)
Async XLA Ops:
  22.8 14.4 %collective-permute-start.3 = (bf16[224,1024]{1,0:T(8,128)(2,1)S(1)}, bf16[224,1024]{1,0:T(8,128)(2,1)S(1)}, u32[]{:S(2)}, u32[]{:S(2)}) collective-permute-start(bf16[224,1024]{1,0:T(8,128)(2,1)S(1)} %get-tuple-element.79.refs_0_), channel_id=1, source_target_pairs={{0,4},{4,8},{8,12},{12,14},{14,10},{10,6},{6,2},{2,0},{1,5},{5,9},... | collective-permute-start | bytes 1376264 | tf_op jit(solution)/shard_map/ppermute | solution.py:294
  24.9 14.4 %collective-permute-start.4 = (bf16[224,1024]{1,0:T(8,128)(2,1)S(1)}, bf16[224,1024]{1,0:T(8,128)(2,1)S(1)}, u32[]{:S(2)}, u32[]{:S(2)}) collective-permute-start(bf16[224,1024]{1,0:T(8,128)(2,1)S(1)} %get-tuple-element.74), channel_id=1, source_target_pairs={{0,2},{4,0},{8,4},{12,8},{14,12},{10,14},{6,10},{2,6},{1,3},{5,1},... | collective-permute-start | bytes 1376264 | tf_op jit(solution)/shard_map/ppermute | solution.py:294
  30.5 15.3 %collective-permute-start.9 = (bf16[224,896]{1,0:T(8,128)(2,1)S(1)}, bf16[224,896]{1,0:T(8,128)(2,1)S(1)}, u32[]{:S(2)}, u32[]{:S(2)}) collective-permute-start(bf16[224,896]{1,0:T(8,128)(2,1)S(1)} %get-tuple-element.80.refs_0_), channel_id=1, source_target_pairs={{0,4},{4,8},{8,12},{12,14},{14,10},{10,6},{6,2},{2,0},{1,5},{5,9},... | collective-permute-start | bytes 1204232 | tf_op jit(solution)/shard_map/ppermute | solution.py:294
  32.2 15.8 %collective-permute-start.10 = (bf16[224,896]{1,0:T(8,128)(2,1)S(1)}, bf16[224,896]{1,0:T(8,128)(2,1)S(1)}, u32[]{:S(2)}, u32[]{:S(2)}) collective-permute-start(bf16[224,896]{1,0:T(8,128)(2,1)S(1)} %get-tuple-element.84), channel_id=1, source_target_pairs={{0,2},{4,0},{8,4},{12,8},{14,12},{10,14},{6,10},{2,6},{1,3},{5,1},... | collective-permute-start | bytes 1204232 | tf_op jit(solution)/shard_map/ppermute | solution.py:294
  40.5 15.1 %collective-permute-start.7 = (bf16[224,1024]{1,0:T(8,128)(2,1)S(1)}, bf16[224,1024]{1,0:T(8,128)(2,1)S(1)}, u32[]{:S(2)}, u32[]{:S(2)}) collective-permute-start(bf16[224,1024]{1,0:T(8,128)(2,1)S(1)} %get-tuple-element.85.refs_0_), channel_id=1, source_target_pairs={{0,4},{4,8},{8,12},{12,14},{14,10},{10,6},{6,2},{2,0},{1,5},{5,9},... | collective-permute-start | bytes 1376264 | tf_op jit(solution)/shard_map/ppermute | solution.py:294
  42.2 15.6 %collective-permute-start.8 = (bf16[224,1024]{1,0:T(8,128)(2,1)S(1)}, bf16[224,1024]{1,0:T(8,128)(2,1)S(1)}, u32[]{:S(2)}, u32[]{:S(2)}) collective-permute-start(bf16[224,1024]{1,0:T(8,128)(2,1)S(1)} %get-tuple-element.82), channel_id=1, source_target_pairs={{0,2},{4,0},{8,4},{12,8},{14,12},{10,14},{6,10},{2,6},{1,3},{5,1},... | collective-permute-start | bytes 1376264 | tf_op jit(solution)/shard_map/ppermute | solution.py:294
  49.0 15.2 %collective-permute-start.13 = (bf16[224,896]{1,0:T(8,128)(2,1)S(1)}, bf16[224,896]{1,0:T(8,128)(2,1)S(1)}, u32[]{:S(2)}, u32[]{:S(2)}) collective-permute-start(bf16[224,896]{1,0:T(8,128)(2,1)S(1)} %get-tuple-element.86.refs_0_), channel_id=1, source_target_pairs={{0,4},{4,8},{8,12},{12,14},{14,10},{10,6},{6,2},{2,0},{1,5},{5,9},... | collective-permute-start | bytes 1204232 | tf_op jit(solution)/shard_map/ppermute | solution.py:294
  50.7 15.7 %collective-permute-start.14 = (bf16[224,896]{1,0:T(8,128)(2,1)S(1)}, bf16[224,896]{1,0:T(8,128)(2,1)S(1)}, u32[]{:S(2)}, u32[]{:S(2)}) collective-permute-start(bf16[224,896]{1,0:T(8,128)(2,1)S(1)} %get-tuple-element.90), channel_id=1, source_target_pairs={{0,2},{4,0},{8,4},{12,8},{14,12},{10,14},{6,10},{2,6},{1,3},{5,1},... | collective-permute-start | bytes 1204232 | tf_op jit(solution)/shard_map/ppermute | solution.py:294
  59.0 15.1 %collective-permute-start.11 = (bf16[224,1024]{1,0:T(8,128)(2,1)S(1)}, bf16[224,1024]{1,0:T(8,128)(2,1)S(1)}, u32[]{:S(2)}, u32[]{:S(2)}) collective-permute-start(bf16[224,1024]{1,0:T(8,128)(2,1)S(1)} %get-tuple-element.91.refs_0_), channel_id=1, source_target_pairs={{0,4},{4,8},{8,12},{12,14},{14,10},{10,6},{6,2},{2,0},{1,5},{5,9},... | collective-permute-start | bytes 1376264 | tf_op jit(solution)/shard_map/ppermute | solution.py:294
  60.6 15.6 %collective-permute-start.12 = (bf16[224,1024]{1,0:T(8,128)(2,1)S(1)}, bf16[224,1024]{1,0:T(8,128)(2,1)S(1)}, u32[]{:S(2)}, u32[]{:S(2)}) collective-permute-start(bf16[224,1024]{1,0:T(8,128)(2,1)S(1)} %get-tuple-element.88), channel_id=1, source_target_pairs={{0,2},{4,0},{8,4},{12,8},{14,12},{10,14},{6,10},{2,6},{1,3},{5,1},... | collective-permute-start | bytes 1376264 | tf_op jit(solution)/shard_map/ppermute | solution.py:294
  67.4 15.3 %collective-permute-start.17 = (bf16[224,896]{1,0:T(8,128)(2,1)S(1)}, bf16[224,896]{1,0:T(8,128)(2,1)S(1)}, u32[]{:S(2)}, u32[]{:S(2)}) collective-permute-start(bf16[224,896]{1,0:T(8,128)(2,1)S(1)} %get-tuple-element.92.refs_0_), channel_id=1, source_target_pairs={{0,4},{4,8},{8,12},{12,14},{14,10},{10,6},{6,2},{2,0},{1,5},{5,9},... | collective-permute-start | bytes 1204232 | tf_op jit(solution)/shard_map/ppermute | solution.py:294
  69.1 15.7 %collective-permute-start.18 = (bf16[224,896]{1,0:T(8,128)(2,1)S(1)}, bf16[224,896]{1,0:T(8,128)(2,1)S(1)}, u32[]{:S(2)}, u32[]{:S(2)}) collective-permute-start(bf16[224,896]{1,0:T(8,128)(2,1)S(1)} %get-tuple-element.96), channel_id=1, source_target_pairs={{0,2},{4,0},{8,4},{12,8},{14,12},{10,14},{6,10},{2,6},{1,3},{5,1},... | collective-permute-start | bytes 1204232 | tf_op jit(solution)/shard_map/ppermute | solution.py:294
  76.7 15.9 %collective-permute-start.15 = (bf16[224,1024]{1,0:T(8,128)(2,1)S(1)}, bf16[224,1024]{1,0:T(8,128)(2,1)S(1)}, u32[]{:S(2)}, u32[]{:S(2)}) collective-permute-start(bf16[224,1024]{1,0:T(8,128)(2,1)S(1)} %shard_map.25.refs_0_.refs_2_), channel_id=1, source_target_pairs={{0,4},{4,8},{8,12},{12,14},{14,10},{10,6},{6,2},{2,0},{1,5},{5,9},... | collective-permute-start | bytes 1376264 | tf_op jit(solution)/shard_map/ppermute | solution.py:294
  78.3 16.3 %collective-permute-start.16 = (bf16[224,1024]{1,0:T(8,128)(2,1)S(1)}, bf16[224,1024]{1,0:T(8,128)(2,1)S(1)}, u32[]{:S(2)}, u32[]{:S(2)}) collective-permute-start(bf16[224,1024]{1,0:T(8,128)(2,1)S(1)} %shard_map.25.refs_0_.refs_2_), channel_id=1, source_target_pairs={{0,2},{4,0},{8,4},{12,8},{14,12},{10,14},{6,10},{2,6},{1,3},{5,1},... | collective-permute-start | bytes 1376264 | tf_op jit(solution)/shard_map/ppermute | solution.py:294
  85.2 16.0 %collective-permute-start.21 = (bf16[224,896]{1,0:T(8,128)(2,1)S(1)}, bf16[224,896]{1,0:T(8,128)(2,1)S(1)}, u32[]{:S(2)}, u32[]{:S(2)}) collective-permute-start(bf16[224,896]{1,0:T(8,128)(2,1)S(1)} %shard_map.26.refs_2_.refs_11_), channel_id=1, source_target_pairs={{0,4},{4,8},{8,12},{12,14},{14,10},{10,6},{6,2},{2,0},{1,5},{5,9},... | collective-permute-start | bytes 1204232 | tf_op jit(solution)/shard_map/ppermute | solution.py:294
  86.8 16.4 %collective-permute-start.22 = (bf16[224,896]{1,0:T(8,128)(2,1)S(1)}, bf16[224,896]{1,0:T(8,128)(2,1)S(1)}, u32[]{:S(2)}, u32[]{:S(2)}) collective-permute-start(bf16[224,896]{1,0:T(8,128)(2,1)S(1)} %shard_map.26.refs_2_.refs_11_), channel_id=1, source_target_pairs={{0,2},{4,0},{8,4},{12,8},{14,12},{10,14},{6,10},{2,6},{1,3},{5,1},... | collective-permute-start | bytes 1204232 | tf_op jit(solution)/shard_map/ppermute | solution.py:294
  94.6 16.3 %collective-permute-start.19 = (bf16[224,1024]{1,0:T(8,128)(2,1)S(1)}, bf16[224,1024]{1,0:T(8,128)(2,1)S(1)}, u32[]{:S(2)}, u32[]{:S(2)}) collective-permute-start(bf16[224,1024]{1,0:T(8,128)(2,1)S(1)} %get-tuple-element.97.refs_2_.refs_3_), channel_id=1, source_target_pairs={{0,4},{4,8},{8,12},{12,14},{14,10},{10,6},{6,2},{2,0},{1,5},{5,9},... | collective-permute-start | bytes 1376264 | tf_op jit(solution)/shard_map/ppermute | solution.py:294
  96.2 16.7 %collective-permute-start.20 = (bf16[224,1024]{1,0:T(8,128)(2,1)S(1)}, bf16[224,1024]{1,0:T(8,128)(2,1)S(1)}, u32[]{:S(2)}, u32[]{:S(2)}) collective-permute-start(bf16[224,1024]{1,0:T(8,128)(2,1)S(1)} %get-tuple-element.98.refs_4_), channel_id=1, source_target_pairs={{0,2},{4,0},{8,4},{12,8},{14,12},{10,14},{6,10},{2,6},{1,3},{5,1},... | collective-permute-start | bytes 1376264 | tf_op jit(solution)/shard_map/ppermute | solution.py:294
  96.7 16.7 %collective-permute-start.33 = (bf16[224,1024]{1,0:T(8,128)(2,1)S(1)}, bf16[224,1024]{1,0:T(8,128)(2,1)S(1)}, u32[]{:S(2)}, u32[]{:S(2)}) collective-permute-start(bf16[224,1024]{1,0:T(8,128)(2,1)S(1)} %shard_map.25.refs_0_.refs_2_), channel_id=1, source_target_pairs={{0,1},{1,0},{2,3},{3,2},{4,5},{5,4},{6,7},{7,6},{8,9},{9,8},{10,11... | collective-permute-start | bytes 1376264 | tf_op jit(solution)/shard_map/ppermute | solution.py:350
  103.2 16.3 %collective-permute-start.25 = (bf16[224,896]{1,0:T(8,128)(2,1)S(1)}, bf16[224,896]{1,0:T(8,128)(2,1)S(1)}, u32[]{:S(2)}, u32[]{:S(2)}) collective-permute-start(bf16[224,896]{1,0:T(8,128)(2,1)S(1)} %get-tuple-element.103.refs_2_.refs_12_), channel_id=1, source_target_pairs={{0,4},{4,8},{8,12},{12,14},{14,10},{10,6},{6,2},{2,0},{1,5},{5,9},... | collective-permute-start | bytes 1204232 | tf_op jit(solution)/shard_map/ppermute | solution.py:294
  113.0 16.4 %collective-permute-start.23 = (bf16[224,1024]{1,0:T(8,128)(2,1)S(1)}, bf16[224,1024]{1,0:T(8,128)(2,1)S(1)}, u32[]{:S(2)}, u32[]{:S(2)}) collective-permute-start(bf16[224,1024]{1,0:T(8,128)(2,1)S(1)} %get-tuple-element.104.refs_2_.refs_5_), channel_id=1, source_target_pairs={{0,4},{4,8},{8,12},{12,14},{14,10},{10,6},{6,2},{2,0},{1,5},{5,9},... | collective-permute-start | bytes 1376264 | tf_op jit(solution)/shard_map/ppermute | solution.py:294
  122.3 15.0 %collective-permute-start.29 = (bf16[224,896]{1,0:T(8,128)(2,1)S(1)}, bf16[224,896]{1,0:T(8,128)(2,1)S(1)}, u32[]{:S(2)}, u32[]{:S(2)}) collective-permute-start(bf16[224,896]{1,0:T(8,128)(2,1)S(1)} %get-tuple-element.110.refs_2_.refs_14_), channel_id=1, source_target_pairs={{0,4},{4,8},{8,12},{12,14},{14,10},{10,6},{6,2},{2,0},{1,5},{5,9},... | collective-permute-start | bytes 1204232 | tf_op jit(solution)/shard_map/ppermute | solution.py:294
  131.5 15.2 %collective-permute-start.45 = (bf16[224,896]{1,0:T(8,128)(2,1)S(1)}, bf16[224,896]{1,0:T(8,128)(2,1)S(1)}, u32[]{:S(2)}, u32[]{:S(2)}) collective-permute-start(bf16[224,896]{1,0:T(8,128)(2,1)S(1)} %get-tuple-element.110.refs_2_.refs_14_), channel_id=1, source_target_pairs={{0,1},{1,0},{2,3},{3,2},{4,5},{5,4},{6,7},{7,6},{8,9},{9,8},{10,11... | collective-permute-start | bytes 1204232 | tf_op jit(solution)/shard_map/ppermute | solution.py:350
  132.1 14.7 %collective-permute-start.37 = (bf16[224,1024]{1,0:T(8,128)(2,1)S(1)}, bf16[224,1024]{1,0:T(8,128)(2,1)S(1)}, u32[]{:S(2)}, u32[]{:S(2)}) collective-permute-start(bf16[224,1024]{1,0:T(8,128)(2,1)S(1)} %get-tuple-element.105.refs_6_), channel_id=1, source_target_pairs={{0,1},{1,0},{2,3},{3,2},{4,5},{5,4},{6,7},{7,6},{8,9},{9,8},{10,11... | collective-permute-start | bytes 1376264 | tf_op jit(solution)/shard_map/ppermute | solution.py:350
  (67 other events, 537.7 us)
